TPU v7x, 32 devices: a whole 2x2x4 slice. The times are simulated.
32 devices in a mesh: gx: 4 (over z), gy: 4 (over x, core), ga: 2 (over y).
Axes of the slice: x: 2, y: 2, z: 4, core: 2. Of those that a mesh axis runs over, the one named last changes fastest.
Arguments:
- velocity: float32 [2, 80, 64, 512], P(None, None, ('gy', 'ga'), 'gx'), may hold values from -4 to 4
- tracers: float32 [2, 80, 64, 512], P(None, None, ('gy', 'ga'), 'gx'), may hold values from -6 to 6
- mixing: float32 [80, 64, 512], P(None, ('gy', 'ga'), 'gx'), may hold values from 0.05 to 400
- thickness: float32 [80], replicated, may hold values from 0.5 to 4
- coriolis: float32 [64], P(('gy', 'ga')), may hold values from -1.5 to 1.5
- land: int32 [64, 512], P(('gy', 'ga'), 'gx'), may hold values 0 or 1
- bottom: int32 [64, 512], P(('gy', 'ga'), 'gx'), may hold values from 70 to 80
- surface: float32 [64, 512], P(('gy', 'ga'), 'gx'), may hold values from -4 to 4
- barotropic: float32 [2, 64, 512], P(None, ('gy', 'ga'), 'gx'), may hold values from -3 to 3
Outputs:
- new_velocity: float32 [2, 80, 64, 512], P(None, None, ('gy', 'ga'), 'gx')
- new_tracers: float32 [2, 80, 64, 512], P(None, None, ('gy', 'ga'), 'gx')
- new_surface: float32 [64, 512], P(('gy', 'ga'), 'gx')
- new_barotropic: float32 [2, 64, 512], P(None, ('gy', 'ga'), 'gx')
All inputs are finite; a program needn't handle non-finite values. No bound on the sum of `land` on one device may be relied on, other than what follows from the above.
Results may differ from a plain program's by a relative error of at most 0.0003.
Values sent between devices are 32-bit elements; how exact they have to be, the bound alone decides.
A program may use at most 64 MiB of HBM per device.

v0:
```python
import functools
import jax
import jax.numpy as jnp
from jax import lax
from jax.experimental import pallas as pl
from jax.experimental.pallas import tpu as pltpu
from jax.sharding import PartitionSpec as P

NSUB = 30
F32 = jnp.float32
MESH = pl.DeviceIdType.MESH
CHUNKS = 5


def kernel(
    nx, ngy, nga, levels,
    vel, trc, mix, dz, cor, land, bot, surf, baro,
    vel_out, trc_out, surf_out, baro_out,
    ynorth, ysouth, hnorth, hsouth,
    xpack, xrecv, crn, crs, bq, bl, bcorn,
    tile2, t2recv, wide1, all1, push1, p2recv, wide2, all2,
    ratio_buf, val_buf, send_sem, recv_sem,
):
    tiles = ngy * nga
    groups = xpack.shape[1]
    per_chunk = levels // CHUNKS
    gx = lax.axis_index("gx")
    t = lax.axis_index("gy") * nga + lax.axis_index("ga")
    left = lax.rem(gx + nx - 1, nx)
    right = lax.rem(gx + 1, nx)
    has_n = t < tiles - 1
    has_s = t > 0

    def dev(x, tile):
        return {"gx": x, "gy": tile // nga, "ga": lax.rem(tile, nga)}

    up = jnp.minimum(t + 1, tiles - 1)
    down = jnp.maximum(t - 1, 0)

    barrier = pltpu.get_barrier_semaphore()

    def greet(d):
        pl.semaphore_signal(barrier, inc=1, device_id=d, device_id_type=MESH)

    greet(dev(left, t))
    greet(dev(right, t))
    for p in range(1, tiles):
        greet(dev(gx, lax.rem(t + p, tiles)))

    @pl.when(has_n)
    def _():
        greet(dev(left, up))
        greet(dev(right, up))

    @pl.when(has_s)
    def _():
        greet(dev(left, down))
        greet(dev(right, down))

    row = lax.broadcasted_iota(jnp.int32, (8, 128), 0)
    lane = lax.broadcasted_iota(jnp.int32, (8, 128), 1)
    slot = lane // 4
    l4 = lane - 4 * slot
    first_l, last_l = lane == 0, lane == 127
    first_r, last_r = row == 0, row == 7

    land_i = land[...]
    be = jnp.where(land_i > 0, bot[...], -1).astype(F32)
    land_f = land_i.astype(F32)

    def depth_body(k, acc):
        total, depth = acc
        d = dz[k]
        wet = jnp.where(k.astype(F32) < be, 1.0, 0.0)
        return total + d, depth + d * wet

    dz_total, depth_sum = lax.fori_loop(
        0, levels, depth_body, (jnp.float32(0.0), jnp.zeros((8, 128), F32))
    )
    safe = jnp.maximum(depth_sum, 1.0)
    rot = jnp.zeros((8, 128), F32)
    for r in range(8):
        rot = jnp.where(row == r, cor[r], rot)
    tile2[0] = surf[...]
    tile2[1] = baro[0]
    tile2[2] = baro[1]
    tile2[3] = be
    tile2[4] = depth_sum / jnp.broadcast_to(dz_total, (8, 128))
    tile2[5] = rot

    pl.semaphore_wait(
        barrier, 2 + tiles - 1 + jnp.where(has_n, 2, 0) + jnp.where(has_s, 2, 0)
    )

    def rc(src, dst, i, d):
        return pltpu.make_async_remote_copy(
            src_ref=src, dst_ref=dst, send_sem=send_sem.at[i], recv_sem=recv_sem.at[i],
            device_id=d, device_id_type=MESH,
        )

    index = [0]

    def nxt():
        index[0] += 1
        return index[0] - 1

    def rows_of(tile):
        return pl.ds(pl.multiple_of(tile * 8, 8), 8)

    def pair(src, recv):
        return [
            rc(src, recv.at[0], nxt(), dev(right, t)),
            rc(src, recv.at[1], nxt(), dev(left, t)),
        ]

    def peers(src, dst):
        starts, waits = [], []
        for p in range(1, tiles):
            i = nxt()
            to = lax.rem(t + p, tiles)
            origin = lax.rem(t + tiles - p, tiles)
            starts.append(rc(src, dst.at[:, rows_of(t), :], i, dev(gx, to)))
            waits.append(rc(src, dst.at[:, rows_of(origin), :], i, dev(gx, to)))
        return starts, waits

    two_d = pair(tile2, t2recv)
    for c in two_d:
        c.start()

    @pl.when(jnp.logical_not(has_n))
    def _():
        hnorth[...] = jnp.zeros_like(hnorth)
        crn[...] = jnp.zeros_like(crn)

    @pl.when(jnp.logical_not(has_s))
    def _():
        hsouth[...] = jnp.zeros_like(hsouth)
        crs[...] = jnp.zeros_like(crs)

    xpack[...] = jnp.zeros_like(xpack)

    def field(c, k):
        return vel[c, k] if c < 2 else trc[c - 2, k]

    def pack_body(k, carry):
        wet = k.astype(F32) < be
        g = k // 32
        m = k - 32 * g
        q = [jnp.where(wet, field(c, k), 0.0) for c in range(4)]
        yn = jnp.concatenate([a[6:8] for a in q], axis=0)
        ys = jnp.concatenate([a[0:2] for a in q], axis=0)
        ynorth[k] = yn
        ysouth[k] = ys
        here = slot == m
        for c, a in enumerate(q + [yn, ys]):
            xpack[c, g] = jnp.where(here, pltpu.roll(a, 2 + 4 * m, 1), xpack[c, g])
        return carry

    to_north, to_south = [], []
    for n in range(CHUNKS):
        span = pl.ds(n * per_chunk, per_chunk)
        lax.fori_loop(n * per_chunk, (n + 1) * per_chunk, pack_body, 0)
        to_north.append(rc(ynorth.at[span], hsouth.at[span], nxt(), dev(gx, up)))
        to_south.append(rc(ysouth.at[span], hnorth.at[span], nxt(), dev(gx, down)))
        pl.when(has_n)(to_north[-1].start)
        pl.when(has_s)(to_south[-1].start)

    x_copies = pair(xpack.at[pl.ds(0, 4)], xrecv)
    for c in x_copies:
        c.start()
    diag_n = [
        rc(xpack.at[4], crs.at[1], nxt(), dev(left, up)),
        rc(xpack.at[4], crs.at[0], nxt(), dev(right, up)),
    ]
    diag_s = [
        rc(xpack.at[5], crn.at[1], nxt(), dev(left, down)),
        rc(xpack.at[5], crn.at[0], nxt(), dev(right, down)),
    ]
    for c in diag_n:
        pl.when(has_n)(c.start)
    for c in diag_s:
        pl.when(has_s)(c.start)

    for c in two_d:
        c.wait_recv()
    for f in range(6):
        wide1[f, :, 0:128] = tile2[f]
        wide1[f, :, 128:256] = jnp.where(lane < 64, t2recv[1, f], t2recv[0, f])
    starts1, waits1 = peers(wide1, all1)
    for c in starts1:
        c.start()
    all1[:, rows_of(t), :] = wide1[...]

    be_side = jnp.where(
        l4 == 1,
        jnp.broadcast_to(t2recv[0, 3][:, 127:128], (8, 128)),
        jnp.broadcast_to(t2recv[1, 3][:, 0:1], (8, 128)),
    )
    for c in x_copies:
        c.wait_recv()
    for c in diag_n:
        pl.when(has_s)(c.wait_recv)
    for c in diag_s:
        pl.when(has_n)(c.wait_recv)

    def close(a):
        return jnp.where(l4 == 1, a, pltpu.roll(a, 126, 1))

    low = l4 < 2
    for g in range(groups):
        corner_n = jnp.where(low, crn[0, g], crn[1, g])
        corner_s = jnp.where(low, crs[0, g], crs[1, g])
        bcorn[0, g] = close(corner_n)
        bcorn[1, g] = close(corner_s)
        wet = (32 * g + slot).astype(F32) < be_side
        for c in range(4):
            a = jnp.where(low, xrecv[0, c, g], xrecv[1, c, g])
            mine = xpack[c, g]
            sides = jnp.where(
                l4 == 1,
                pltpu.roll(a, 1, 1) + pltpu.roll(mine, 127, 1),
                pltpu.roll(a, 127, 1) + pltpu.roll(mine, 1, 1),
            )
            north = jnp.where(
                last_r, jnp.broadcast_to(corner_n[2 * c:2 * c + 1], (8, 128)), pltpu.roll(a, 7, 0)
            )
            south = jnp.where(
                first_r, jnp.broadcast_to(corner_s[2 * c + 1:2 * c + 2], (8, 128)), pltpu.roll(a, 1, 0)
            )
            lap = jnp.where(wet, sides + north + south - 4.0 * a, 0.0)
            bq[c, g] = close(a)
            bl[c, g] = close(lap)

    for c in waits1:
        c.wait_recv()
    be_n = jnp.where(
        has_n, jnp.broadcast_to(all1[3, rows_of(up), 0:128][0:1], (8, 128)), -1.0
    )
    be_s = jnp.where(
        has_s, jnp.broadcast_to(all1[3, rows_of(down), 0:128][7:8], (8, 128)), -1.0
    )

    def east_west(a, h):
        return (
            jnp.where(last_l, h, pltpu.roll(a, 127, 1)),
            jnp.where(first_l, h, pltpu.roll(a, 1, 1)),
        )

    def row_of(a, r):
        return jnp.broadcast_to(a[r:r + 1], (8, 128))

    def level_body(k, carry):
        acc_x, acc_y, force_u, force_v, e_up, ratio, values = carry
        kf = k.astype(F32)
        d = dz[k]
        k_next = jnp.minimum(k + 1, levels - 1)
        d_next = dz[k_next]
        g = k // 32
        turn = 127 - 4 * (k - 32 * g)
        wet = kf < be
        wet_next = jnp.logical_and(kf + 1.0 < be, k + 1 < levels)
        q = [jnp.where(wet, field(c, k), 0.0) for c in range(4)]
        hn, hs = hnorth[k], hsouth[k]
        he, hw = east_west(hn, pltpu.roll(bcorn[0, g], turn, 1))
        lap_n = jnp.where(
            kf < be_n, pltpu.roll(hn + ynorth[k], 7, 0) + he + hw - 4.0 * hn, 0.0
        )
        he, hw = east_west(hs, pltpu.roll(bcorn[1, g], turn, 1))
        lap_s = jnp.where(
            kf < be_s, pltpu.roll(hs + ysouth[k], 1, 0) + he + hw - 4.0 * hs, 0.0
        )
        around, smooth = [], []
        for c in range(4):
            a = q[c]
            e, w = east_west(a, pltpu.roll(bq[c, g], turn, 1))
            n = jnp.where(last_r, row_of(hn, 2 * c), pltpu.roll(a, 7, 0))
            s = jnp.where(first_r, row_of(hs, 2 * c + 1), pltpu.roll(a, 1, 0))
            around.append((e, w, n, s))
            lap = jnp.where(wet, (e + w) + (n + s) - 4.0 * a, 0.0)
            e, w = east_west(lap, pltpu.roll(bl[c, g], turn, 1))
            n = jnp.where(last_r, row_of(lap_n, 2 * c), pltpu.roll(lap, 7, 0))
            s = jnp.where(first_r, row_of(lap_s, 2 * c + 1), pltpu.roll(lap, 1, 0))
            smooth.append(0.02 * ((e + w) + (n + s) - 4.0 * lap))
        weights = [
            (0.1 * around[3][i] - 0.2 * around[2][i]) * d for i in range(4)
        ]
        slope_x = weights[0] - weights[1]
        slope_y = weights[2] - weights[3]
        press_x = 0.01 * (acc_x + 0.5 * slope_x)
        press_y = 0.01 * (acc_y + 0.5 * slope_y)
        acc_x = acc_x + slope_x
        acc_y = acc_y + slope_y
        ue, uw = around[0][0], around[0][1]
        vn, vs = around[1][2], around[1][3]
        extra = [rot * q[1] - press_x, -rot * q[0] - press_y, 0.0, 0.0]
        growth = []
        for c in range(4):
            e, w, n, s = around[c]
            advect = 0.5 * ((ue * e - uw * w) + (vn * n - vs * s))
            growth.append(jnp.where(wet, extra[c] - smooth[c] - advect, 0.0))
        force_u = force_u + d * growth[0]
        force_v = force_v + d * growth[1]
        e_now = jnp.where(
            jnp.logical_and(wet, wet_next), mix[k] / (0.5 * (d + d_next)), 0.0
        )
        inverse = 1.0 / (d + e_up + e_now - e_up * ratio)
        ratio = e_now * inverse
        ratio_buf[k] = ratio
        new_values = []
        for c in range(4):
            val = (d * (q[c] + 0.1 * growth[c]) + e_up * values[c]) * inverse
            val_buf[c, k] = val
            new_values.append(val)
        return acc_x, acc_y, force_u, force_v, e_now, ratio, tuple(new_values)

    zero = jnp.zeros((8, 128), F32)
    carry = (zero, zero, zero, zero, zero, zero, (zero, zero, zero, zero))
    for n in range(CHUNKS):
        pl.when(has_s)(to_north[n].wait_recv)
        pl.when(has_n)(to_south[n].wait_recv)
        carry = lax.fori_loop(n * per_chunk, (n + 1) * per_chunk, level_body, carry)

    scale = land_f / safe
    push1[0] = carry[2] * scale
    push1[1] = carry[3] * scale
    push_copies = pair(push1, p2recv)
    for c in push_copies:
        c.start()

    def back_body(i, state):
        after, mean_u, mean_v = state
        k = levels - 1 - i
        ratio = ratio_buf[k]
        now = [val_buf[c, k] + ratio * after[c] for c in range(4)]
        val_buf[0, k] = now[0]
        val_buf[1, k] = now[1]
        trc_out[0, k] = now[2]
        trc_out[1, k] = now[3]
        part = jnp.where(k.astype(F32) < be, dz[k], 0.0)
        return tuple(now), mean_u + part * now[0], mean_v + part * now[1]

    half = levels // 4
    state = lax.fori_loop(0, half, back_body, ((zero,) * 4, zero, zero))
    for c in push_copies:
        c.wait_recv()
    for f in range(2):
        wide2[f, :, 0:128] = push1[f]
        wide2[f, :, 128:256] = jnp.where(lane < 64, p2recv[1, f], p2recv[0, f])
    starts2, waits2 = peers(wide2, all2)
    for c in starts2:
        c.start()
    all2[:, rows_of(t), :] = wide2[...]
    state = lax.fori_loop(half, levels, back_body, state)
    unused, mean_u, mean_v = state

    shape = (8 * tiles, 256)
    rows = lax.broadcasted_iota(jnp.int32, shape, 0)
    top, base = rows == shape[0] - 1, rows == 0
    sea = jnp.where(all1[3] >= 0.0, 1.0, 0.0)
    ratio_x = 0.05 * all1[4]
    for c in waits2:
        c.wait_recv()
    all1[3] = sea
    all1[4] = ratio_x
    all1[5] = 0.1 * all1[5] * sea
    all2[0] = 0.1 * all2[0] * sea
    all2[1] = 0.1 * all2[1] * sea
    mine = rows_of(t)

    def diff_x(a):
        return pltpu.roll(a, 255, 1) - pltpu.roll(a, 1, 1)

    def diff_y(a):
        return jnp.where(top, 0.0, pltpu.roll(a, shape[0] - 1, 0)) - jnp.where(
            base, 0.0, pltpu.roll(a, 1, 0)
        )

    def sub_body(i, sums):
        height, u, v = all1[0], all1[1], all1[2]
        sea, dr, f = all1[3], all1[4], all1[5]
        height = (height - (diff_x(dr * u) + diff_y(dr * v))) * sea
        g = 1.25 * sea
        new_u = u * sea + all2[0] + f * v - g * diff_x(height)
        new_v = v * sea + all2[1] - f * u - g * diff_y(height)
        all1[0] = height
        all1[1] = new_u
        all1[2] = new_v
        return sums[0] + all1[1, mine, 0:128], sums[1] + all1[2, mine, 0:128]

    sum_u, sum_v = lax.fori_loop(0, NSUB, sub_body, (zero, zero))
    surf_out[...] = all1[0, mine, 0:128]
    baro_out[0] = all1[1, mine, 0:128]
    baro_out[1] = all1[2, mine, 0:128]
    shift_u = sum_u * (1.0 / NSUB) - mean_u / safe
    shift_v = sum_v * (1.0 / NSUB) - mean_v / safe

    def out_body(k, carry):
        wet = k.astype(F32) < be
        vel_out[0, k] = jnp.where(wet, val_buf[0, k] + shift_u, 0.0)
        vel_out[1, k] = jnp.where(wet, val_buf[1, k] + shift_v, 0.0)
        return carry

    lax.fori_loop(0, levels, out_body, 0)

    for c in two_d + x_copies + starts1 + push_copies + starts2:
        c.wait_send()
    for c in to_north + diag_n:
        pl.when(has_n)(c.wait_send)
    for c in to_south + diag_s:
        pl.when(has_s)(c.wait_send)


def shards(nx, ngy, nga, velocity, tracers, mixing, thickness, coriolis, land, bottom, surface, barotropic):
    levels = thickness.shape[0]
    tiles = ngy * nga
    groups = (levels + 31) // 32
    copies = 2 + 2 * CHUNKS + 2 + 4 + (tiles - 1) + 2 + (tiles - 1)
    tile = (8, 128)
    scratch = [
        (levels,) + tile, (levels,) + tile, (levels,) + tile, (levels,) + tile,
        (6, groups) + tile, (2, 4, groups) + tile, (2, groups) + tile, (2, groups) + tile,
        (4, groups) + tile, (4, groups) + tile, (2, groups) + tile,
        (6,) + tile, (2, 6) + tile, (6, 8, 256), (6, 8 * tiles, 256),
        (2,) + tile, (2, 2) + tile, (2, 8, 256), (2, 8 * tiles, 256),
        (levels,) + tile, (4, levels) + tile,
    ]
    vmem = pl.BlockSpec(memory_space=pltpu.VMEM)
    smem = pl.BlockSpec(memory_space=pltpu.SMEM)
    return pl.pallas_call(
        functools.partial(kernel, nx, ngy, nga, levels),
        out_shape=(
            jax.ShapeDtypeStruct(velocity.shape, F32),
            jax.ShapeDtypeStruct(tracers.shape, F32),
            jax.ShapeDtypeStruct(surface.shape, F32),
            jax.ShapeDtypeStruct(barotropic.shape, F32),
        ),
        in_specs=[vmem, vmem, vmem, smem, smem, vmem, vmem, vmem, vmem],
        out_specs=(vmem, vmem, vmem, vmem),
        scratch_shapes=[pltpu.VMEM(s, F32) for s in scratch]
        + [pltpu.SemaphoreType.DMA((copies,)), pltpu.SemaphoreType.DMA((copies,))],
        compiler_params=pltpu.CompilerParams(
            collective_id=0, has_side_effects=True, vmem_limit_bytes=40 * 1024 * 1024
        ),
    )(velocity, tracers, mixing, thickness, coriolis, land, bottom, surface, barotropic)


def solution(mesh):
    sizes = mesh.shape
    return jax.shard_map(
        functools.partial(shards, sizes["gx"], sizes["gy"], sizes["ga"]),
        mesh=mesh,
        in_specs=(
            P(None, None, ("gy", "ga"), "gx"),
            P(None, None, ("gy", "ga"), "gx"),
            P(None, ("gy", "ga"), "gx"),
            P(),
            P(("gy", "ga")),
            P(("gy", "ga"), "gx"),
            P(("gy", "ga"), "gx"),
            P(("gy", "ga"), "gx"),
            P(None, ("gy", "ga"), "gx"),
        ),
        out_specs=(
            P(None, None, ("gy", "ga"), "gx"),
            P(None, None, ("gy", "ga"), "gx"),
            P(("gy", "ga"), "gx"),
            P(None, ("gy", "ga"), "gx"),
        ),
        check_vma=False,
    )
```

profile of v0, /device:TPU:0, one launch (start us, length us, event | category | flops | bytes accessed | tf_op | source)
XLA Modules:
  0.0 67.2 jit_solution(6283245825796940786)
XLA Ops:
  0.6 0.0 copy-start
  0.6 1.1 %copy-done = f32[2,80,8,128]{3,2,1,0:T(8,128)S(1)} copy-done((f32[2,80,8,128]{3,2,1,0:T(8,128)S(1)}, f32[2,80,8,128]{3,2,1,0:T(8,128)}, u32[]{:S(2)}) %copy-start) | copy-done | bytes 655384
  1.7 0.0 copy-start.1
  1.7 1.1 %copy-done.1 = f32[2,80,8,128]{3,2,1,0:T(8,128)S(1)} copy-done((f32[2,80,8,128]{3,2,1,0:T(8,128)S(1)}, f32[2,80,8,128]{3,2,1,0:T(8,128)}, u32[]{:S(2)}) %copy-start.1) | copy-done | bytes 655384
  2.8 0.0 copy-start.2
  2.8 1.0 %copy-done.2 = f32[80,8,128]{2,1,0:T(8,128)S(1)} copy-done((f32[80,8,128]{2,1,0:T(8,128)S(1)}, f32[80,8,128]{2,1,0:T(8,128)}, u32[]{:S(2)}) %copy-start.2) | copy-done | bytes 327704
  3.8 0.0 copy-start.3
  3.8 0.7 %copy-done.3 = f32[2,8,128]{2,1,0:T(8,128)S(1)} copy-done((f32[2,8,128]{2,1,0:T(8,128)S(1)}, f32[2,8,128]{2,1,0:T(8,128)}, u32[]{:S(2)}) %copy-start.3) | copy-done | bytes 8216
  4.5 0.0 copy-start.4
  4.5 0.7 %copy-done.4 = s32[8,128]{1,0:T(8,128)S(1)} copy-done((s32[8,128]{1,0:T(8,128)S(1)}, s32[8,128]{1,0:T(8,128)}, u32[]{:S(2)}) %copy-start.4) | copy-done | bytes 4120
  5.2 0.0 copy-start.5
  5.2 0.7 %copy-done.5 = s32[8,128]{1,0:T(8,128)S(1)} copy-done((s32[8,128]{1,0:T(8,128)S(1)}, s32[8,128]{1,0:T(8,128)}, u32[]{:S(2)}) %copy-start.5) | copy-done | bytes 4120
  5.9 0.0 copy-start.6
  5.9 0.7 %copy-done.6 = f32[8,128]{1,0:T(8,128)S(1)} copy-done((f32[8,128]{1,0:T(8,128)S(1)}, f32[8,128]{1,0:T(8,128)}, u32[]{:S(2)}) %copy-start.6) | copy-done | bytes 4120
  6.5 0.0 copy-start.7
  6.5 0.7 copy-done.7
  7.2 0.0 copy-start.8
  7.2 0.7 copy-done.8
  7.9 56.5 %shard_map.120 = (f32[2,80,8,128]{3,2,1,0:T(8,128)S(1)}, f32[2,80,8,128]{3,2,1,0:T(8,128)S(1)}, f32[8,128]{1,0:T(8,128)S(1)}, f32[2,8,128]{2,1,0:T(8,128)S(1)}) custom-call(f32[2,80,8,128]{3,2,1,0:T(8,128)S(1)} %copy-done, f32[2,80,8,128]{3,2,1,0:T(8,128)S(1)} %copy-done.1, f32[80,8,128]{2,1,0:T(8,128)S(1)} %copy-done.2, f32[80]{0:T(128)S(1)} %copy-done.7, ...), custom_call_target="tpu_custom_call" | custom-call | tf_op jit(solution)/shard_map/pallas_call | solution.py:429
  64.3 0.8 %copy.17 = f32[2,80,8,128]{3,2,1,0:T(8,128)} copy(f32[2,80,8,128]{3,2,1,0:T(8,128)S(1)} %get-tuple-element.8) | data formatting | bytes 1310720
  65.2 0.8 %copy.18 = f32[2,80,8,128]{3,2,1,0:T(8,128)} copy(f32[2,80,8,128]{3,2,1,0:T(8,128)S(1)} %get-tuple-element.9) | data formatting | bytes 1310720
  66.0 0.6 copy.19
  66.6 0.6 copy.20
Async XLA Ops:
  0.6 1.1 %copy-start = (f32[2,80,8,128]{3,2,1,0:T(8,128)S(1)}, f32[2,80,8,128]{3,2,1,0:T(8,128)}, u32[]{:S(2)}) copy-start(f32[2,80,8,128]{3,2,1,0:T(8,128)} %vel.1) | copy-start | bytes 1966084
  1.7 1.1 %copy-start.1 = (f32[2,80,8,128]{3,2,1,0:T(8,128)S(1)}, f32[2,80,8,128]{3,2,1,0:T(8,128)}, u32[]{:S(2)}) copy-start(f32[2,80,8,128]{3,2,1,0:T(8,128)} %trc.1) | copy-start | bytes 1966084
  2.8 1.0 %copy-start.2 = (f32[80,8,128]{2,1,0:T(8,128)S(1)}, f32[80,8,128]{2,1,0:T(8,128)}, u32[]{:S(2)}) copy-start(f32[80,8,128]{2,1,0:T(8,128)} %mix.1) | copy-start | bytes 983044
  3.8 0.7 %copy-start.3 = (f32[2,8,128]{2,1,0:T(8,128)S(1)}, f32[2,8,128]{2,1,0:T(8,128)}, u32[]{:S(2)}) copy-start(f32[2,8,128]{2,1,0:T(8,128)} %baro.1) | copy-start | bytes 24580
  4.5 0.7 %copy-start.4 = (s32[8,128]{1,0:T(8,128)S(1)}, s32[8,128]{1,0:T(8,128)}, u32[]{:S(2)}) copy-start(s32[8,128]{1,0:T(8,128)} %land.1) | copy-start | bytes 12292
  5.2 0.7 %copy-start.5 = (s32[8,128]{1,0:T(8,128)S(1)}, s32[8,128]{1,0:T(8,128)}, u32[]{:S(2)}) copy-start(s32[8,128]{1,0:T(8,128)} %bot.1) | copy-start | bytes 12292
  5.9 0.7 %copy-start.6 = (f32[8,128]{1,0:T(8,128)S(1)}, f32[8,128]{1,0:T(8,128)}, u32[]{:S(2)}) copy-start(f32[8,128]{1,0:T(8,128)} %surf.1) | copy-start | bytes 12292
  6.5 0.7 copy-start.7
  7.2 0.7 copy-start.8
where the time goes:
time: 67.6 us; the launch traced here: 67.2 us
  Pallas kernels  56.5 us (84%)
  local copies, waits for them, and re-layouts  10.1 us (15%)
    pallas_call x1, Pallas kernels, shards(): pl.pallas_call(functools.partial(kernel, nx, ngy, nga, levels), out_shape...  56.5 us
    unnamed x22, local copies, waits for them, and re-layouts  10.1 us

commit v1 on v0

--- a/solution.py
+++ b/solution.py
@@ -9,21 +9,33 @@
 NSUB = 30
 F32 = jnp.float32
 MESH = pl.DeviceIdType.MESH
-CHUNKS = 5
+BLOCK = 8
 
 
 def kernel(
     nx, ngy, nga, levels,
-    vel, trc, mix, dz, cor, land, bot, surf, baro,
+    vel_in, trc_in, mix_in, dz_in, cor_in, land_in, bot_in, surf_in, baro_in,
     vel_out, trc_out, surf_out, baro_out,
     ynorth, ysouth, hnorth, hsouth,
     xpack, xrecv, crn, crs, bq, bl, bcorn,
     tile2, t2recv, wide1, all1, push1, p2recv, wide2, all2,
-    ratio_buf, val_buf, send_sem, recv_sem,
+    ratio_buf, val_buf, be_above, be_below,
+    vel, trc, mix, dz, cor, land, bot, surf, baro,
+    send_sem, recv_sem, load_sem,
 ):
     tiles = ngy * nga
     groups = xpack.shape[1]
-    per_chunk = levels // CHUNKS
+    blocks = levels // BLOCK
+    per_group = 32 // BLOCK
+    loads = [
+        pltpu.make_async_copy(src, dst, load_sem.at[i])
+        for i, (src, dst) in enumerate([
+            (dz_in, dz), (cor_in, cor), (land_in, land), (bot_in, bot), (surf_in, surf),
+            (baro_in, baro), (vel_in, vel), (trc_in, trc), (mix_in, mix),
+        ])
+    ]
+    for c in loads:
+        c.start()
     gx = lax.axis_index("gx")
     t = lax.axis_index("gy") * nga + lax.axis_index("ga")
     left = lax.rem(gx + nx - 1, nx)
@@ -64,18 +76,23 @@
     first_l, last_l = lane == 0, lane == 127
     first_r, last_r = row == 0, row == 7
 
+    for c in loads[:6]:
+        c.wait()
     land_i = land[...]
     be = jnp.where(land_i > 0, bot[...], -1).astype(F32)
     land_f = land_i.astype(F32)
 
-    def depth_body(k, acc):
+    def depth_body(n, acc):
         total, depth = acc
-        d = dz[k]
-        wet = jnp.where(k.astype(F32) < be, 1.0, 0.0)
-        return total + d, depth + d * wet
+        for i in range(BLOCK):
+            k = n * BLOCK + i
+            d = dz[k]
+            total = total + d
+            depth = depth + jnp.where(k.astype(F32) < be, d, 0.0)
+        return total, depth
 
     dz_total, depth_sum = lax.fori_loop(
-        0, levels, depth_body, (jnp.float32(0.0), jnp.zeros((8, 128), F32))
+        0, blocks, depth_body, (jnp.float32(0.0), jnp.zeros((8, 128), F32))
     )
     safe = jnp.maximum(depth_sum, 1.0)
     rot = jnp.zeros((8, 128), F32)
@@ -126,45 +143,53 @@
     two_d = pair(tile2, t2recv)
     for c in two_d:
         c.start()
+    be_up = rc(tile2.at[3], be_below, nxt(), dev(gx, up))
+    be_down = rc(tile2.at[3], be_above, nxt(), dev(gx, down))
+    pl.when(has_n)(be_up.start)
+    pl.when(has_s)(be_down.start)
+    for c in loads[6:8]:
+        c.wait()
 
     @pl.when(jnp.logical_not(has_n))
     def _():
         hnorth[...] = jnp.zeros_like(hnorth)
         crn[...] = jnp.zeros_like(crn)
+        be_above[...] = jnp.full_like(be_above, -1.0)
 
     @pl.when(jnp.logical_not(has_s))
     def _():
         hsouth[...] = jnp.zeros_like(hsouth)
         crs[...] = jnp.zeros_like(crs)
+        be_below[...] = jnp.full_like(be_below, -1.0)
 
     xpack[...] = jnp.zeros_like(xpack)
 
     def field(c, k):
         return vel[c, k] if c < 2 else trc[c - 2, k]
 
-    def pack_body(k, carry):
-        wet = k.astype(F32) < be
-        g = k // 32
-        m = k - 32 * g
-        q = [jnp.where(wet, field(c, k), 0.0) for c in range(4)]
-        yn = jnp.concatenate([a[6:8] for a in q], axis=0)
-        ys = jnp.concatenate([a[0:2] for a in q], axis=0)
-        ynorth[k] = yn
-        ysouth[k] = ys
-        here = slot == m
-        for c, a in enumerate(q + [yn, ys]):
-            xpack[c, g] = jnp.where(here, pltpu.roll(a, 2 + 4 * m, 1), xpack[c, g])
+    def pack_body(n, carry):
+        acc = [jnp.zeros((8, 128), F32)] * 6
+        for i in range(BLOCK):
+            k = n * BLOCK + i
+            wet = k.astype(F32) < be
+            q = [jnp.where(wet, field(c, k), 0.0) for c in range(4)]
+            yn = jnp.concatenate([a[6:8] for a in q], axis=0)
+            ys = jnp.concatenate([a[0:2] for a in q], axis=0)
+            ynorth[k] = yn
+            ysouth[k] = ys
+            here = slot == i
+            for c, a in enumerate(q + [yn, ys]):
+                acc[c] = jnp.where(here, pltpu.roll(a, 2 + 4 * i, 1), acc[c])
+        g = n // per_group
+        part = n - per_group * g
+        here = slot // BLOCK == part
+        for c in range(6):
+            xpack[c, g] = jnp.where(
+                here, pltpu.roll(acc[c], 4 * BLOCK * part, 1), xpack[c, g]
+            )
         return carry
 
-    to_north, to_south = [], []
-    for n in range(CHUNKS):
-        span = pl.ds(n * per_chunk, per_chunk)
-        lax.fori_loop(n * per_chunk, (n + 1) * per_chunk, pack_body, 0)
-        to_north.append(rc(ynorth.at[span], hsouth.at[span], nxt(), dev(gx, up)))
-        to_south.append(rc(ysouth.at[span], hnorth.at[span], nxt(), dev(gx, down)))
-        pl.when(has_n)(to_north[-1].start)
-        pl.when(has_s)(to_south[-1].start)
-
+    lax.fori_loop(0, blocks, pack_body, 0)
     x_copies = pair(xpack.at[pl.ds(0, 4)], xrecv)
     for c in x_copies:
         c.start()
@@ -180,6 +205,21 @@
         pl.when(has_n)(c.start)
     for c in diag_s:
         pl.when(has_s)(c.start)
+
+    first_north, first_south = index[0], index[0] + blocks
+    index[0] += 2 * blocks
+
+    def to_north(n):
+        span = pl.ds(n * BLOCK, BLOCK)
+        return rc(ynorth.at[span], hsouth.at[span], first_north + n, dev(gx, up))
+
+    def to_south(n):
+        span = pl.ds(n * BLOCK, BLOCK)
+        return rc(ysouth.at[span], hnorth.at[span], first_south + n, dev(gx, down))
+
+    for n in range(blocks):
+        pl.when(has_n)(to_north(n).start)
+        pl.when(has_s)(to_south(n).start)
 
     for c in two_d:
         c.wait_recv()
@@ -231,14 +271,11 @@
             bq[c, g] = close(a)
             bl[c, g] = close(lap)
 
-    for c in waits1:
-        c.wait_recv()
-    be_n = jnp.where(
-        has_n, jnp.broadcast_to(all1[3, rows_of(up), 0:128][0:1], (8, 128)), -1.0
-    )
-    be_s = jnp.where(
-        has_s, jnp.broadcast_to(all1[3, rows_of(down), 0:128][7:8], (8, 128)), -1.0
-    )
+    pl.when(has_s)(be_up.wait_recv)
+    pl.when(has_n)(be_down.wait_recv)
+    loads[8].wait()
+    be_n = jnp.broadcast_to(be_above[0:1, :], (8, 128))
+    be_s = jnp.broadcast_to(be_below[7:8, :], (8, 128))
 
     def east_west(a, h):
         return (
@@ -249,35 +286,36 @@
     def row_of(a, r):
         return jnp.broadcast_to(a[r:r + 1], (8, 128))
 
-    def level_body(k, carry):
+    def level(n, i, rims, carry):
+        rim_q, rim_l, rim_c = rims
+        k = n * BLOCK + i
         acc_x, acc_y, force_u, force_v, e_up, ratio, values = carry
         kf = k.astype(F32)
         d = dz[k]
         k_next = jnp.minimum(k + 1, levels - 1)
         d_next = dz[k_next]
-        g = k // 32
-        turn = 127 - 4 * (k - 32 * g)
+        turn = 127 - 4 * i
         wet = kf < be
         wet_next = jnp.logical_and(kf + 1.0 < be, k + 1 < levels)
         q = [jnp.where(wet, field(c, k), 0.0) for c in range(4)]
         hn, hs = hnorth[k], hsouth[k]
-        he, hw = east_west(hn, pltpu.roll(bcorn[0, g], turn, 1))
+        he, hw = east_west(hn, pltpu.roll(rim_c[0], turn, 1))
         lap_n = jnp.where(
             kf < be_n, pltpu.roll(hn + ynorth[k], 7, 0) + he + hw - 4.0 * hn, 0.0
         )
-        he, hw = east_west(hs, pltpu.roll(bcorn[1, g], turn, 1))
+        he, hw = east_west(hs, pltpu.roll(rim_c[1], turn, 1))
         lap_s = jnp.where(
             kf < be_s, pltpu.roll(hs + ysouth[k], 1, 0) + he + hw - 4.0 * hs, 0.0
         )
         around, smooth = [], []
         for c in range(4):
             a = q[c]
-            e, w = east_west(a, pltpu.roll(bq[c, g], turn, 1))
-            n = jnp.where(last_r, row_of(hn, 2 * c), pltpu.roll(a, 7, 0))
-            s = jnp.where(first_r, row_of(hs, 2 * c + 1), pltpu.roll(a, 1, 0))
+            e, w = east_west(a, pltpu.roll(rim_q[c], turn, 1))
+            n = jnp.where(last_r, jnp.broadcast_to(hnorth[k, 2 * c:2 * c + 1, :], (8, 128)), pltpu.roll(a, 7, 0))
+            s = jnp.where(first_r, jnp.broadcast_to(hsouth[k, 2 * c + 1:2 * c + 2, :], (8, 128)), pltpu.roll(a, 1, 0))
             around.append((e, w, n, s))
             lap = jnp.where(wet, (e + w) + (n + s) - 4.0 * a, 0.0)
-            e, w = east_west(lap, pltpu.roll(bl[c, g], turn, 1))
+            e, w = east_west(lap, pltpu.roll(rim_l[c], turn, 1))
             n = jnp.where(last_r, row_of(lap_n, 2 * c), pltpu.roll(lap, 7, 0))
             s = jnp.where(first_r, row_of(lap_s, 2 * c + 1), pltpu.roll(lap, 1, 0))
             smooth.append(0.02 * ((e + w) + (n + s) - 4.0 * lap))
@@ -315,10 +353,22 @@
 
     zero = jnp.zeros((8, 128), F32)
     carry = (zero, zero, zero, zero, zero, zero, (zero, zero, zero, zero))
-    for n in range(CHUNKS):
-        pl.when(has_s)(to_north[n].wait_recv)
-        pl.when(has_n)(to_south[n].wait_recv)
-        carry = lax.fori_loop(n * per_chunk, (n + 1) * per_chunk, level_body, carry)
+
+    def block_body(n, carry):
+        g = n // per_group
+        back = lax.rem(128 - 4 * BLOCK * (n - per_group * g), 128)
+        rims = (
+            [pltpu.roll(bq[c, g], back, 1) for c in range(4)],
+            [pltpu.roll(bl[c, g], back, 1) for c in range(4)],
+            [pltpu.roll(bcorn[c, g], back, 1) for c in range(2)],
+        )
+        pl.when(has_s)(lambda: to_north(n).wait_recv())
+        pl.when(has_n)(lambda: to_south(n).wait_recv())
+        for i in range(BLOCK):
+            carry = level(n, i, rims, carry)
+        return carry
+
+    carry = lax.fori_loop(0, blocks, block_body, carry)
 
     scale = land_f / safe
     push1[0] = carry[2] * scale
@@ -327,19 +377,23 @@
     for c in push_copies:
         c.start()
 
-    def back_body(i, state):
+    def back_body(n, state):
         after, mean_u, mean_v = state
-        k = levels - 1 - i
-        ratio = ratio_buf[k]
-        now = [val_buf[c, k] + ratio * after[c] for c in range(4)]
-        val_buf[0, k] = now[0]
-        val_buf[1, k] = now[1]
-        trc_out[0, k] = now[2]
-        trc_out[1, k] = now[3]
-        part = jnp.where(k.astype(F32) < be, dz[k], 0.0)
-        return tuple(now), mean_u + part * now[0], mean_v + part * now[1]
-
-    half = levels // 4
+        for i in range(BLOCK):
+            k = levels - 1 - n * BLOCK - i
+            ratio = ratio_buf[k]
+            now = [val_buf[c, k] + ratio * after[c] for c in range(4)]
+            val_buf[0, k] = now[0]
+            val_buf[1, k] = now[1]
+            trc_out[0, k] = now[2]
+            trc_out[1, k] = now[3]
+            part = jnp.where(k.astype(F32) < be, dz[k], 0.0)
+            mean_u = mean_u + part * now[0]
+            mean_v = mean_v + part * now[1]
+            after = tuple(now)
+        return after, mean_u, mean_v
+
+    half = blocks // 3
     state = lax.fori_loop(0, half, back_body, ((zero,) * 4, zero, zero))
     for c in push_copies:
         c.wait_recv()
@@ -350,12 +404,14 @@
     for c in starts2:
         c.start()
     all2[:, rows_of(t), :] = wide2[...]
-    state = lax.fori_loop(half, levels, back_body, state)
+    state = lax.fori_loop(half, blocks, back_body, state)
     unused, mean_u, mean_v = state
 
     shape = (8 * tiles, 256)
     rows = lax.broadcasted_iota(jnp.int32, shape, 0)
     top, base = rows == shape[0] - 1, rows == 0
+    for c in waits1:
+        c.wait_recv()
     sea = jnp.where(all1[3] >= 0.0, 1.0, 0.0)
     ratio_x = 0.05 * all1[4]
     for c in waits2:
@@ -394,27 +450,41 @@
     shift_u = sum_u * (1.0 / NSUB) - mean_u / safe
     shift_v = sum_v * (1.0 / NSUB) - mean_v / safe
 
-    def out_body(k, carry):
-        wet = k.astype(F32) < be
-        vel_out[0, k] = jnp.where(wet, val_buf[0, k] + shift_u, 0.0)
-        vel_out[1, k] = jnp.where(wet, val_buf[1, k] + shift_v, 0.0)
+    def out_body(n, carry):
+        for i in range(BLOCK):
+            k = n * BLOCK + i
+            wet = k.astype(F32) < be
+            vel_out[0, k] = jnp.where(wet, val_buf[0, k] + shift_u, 0.0)
+            vel_out[1, k] = jnp.where(wet, val_buf[1, k] + shift_v, 0.0)
         return carry
 
-    lax.fori_loop(0, levels, out_body, 0)
+    lax.fori_loop(0, blocks, out_body, 0)
 
     for c in two_d + x_copies + starts1 + push_copies + starts2:
         c.wait_send()
-    for c in to_north + diag_n:
+    norths = diag_n + [be_up] + [to_north(n) for n in range(blocks)]
+    souths = diag_s + [be_down] + [to_south(n) for n in range(blocks)]
+    for c in norths:
         pl.when(has_n)(c.wait_send)
-    for c in to_south + diag_s:
+    for c in souths:
         pl.when(has_s)(c.wait_send)
+
+
+def settle(*refs):
+    count = len(refs) // 2
+    sem = refs[-1]
+    copies = [pltpu.make_async_copy(refs[i], refs[count + i], sem.at[i]) for i in range(count)]
+    for c in copies:
+        c.start()
+    for c in copies:
+        c.wait()
 
 
 def shards(nx, ngy, nga, velocity, tracers, mixing, thickness, coriolis, land, bottom, surface, barotropic):
     levels = thickness.shape[0]
     tiles = ngy * nga
     groups = (levels + 31) // 32
-    copies = 2 + 2 * CHUNKS + 2 + 4 + (tiles - 1) + 2 + (tiles - 1)
+    copies = 4 + 2 * (levels // BLOCK) + 2 + 4 + (tiles - 1) + 2 + (tiles - 1)
     tile = (8, 128)
     scratch = [
         (levels,) + tile, (levels,) + tile, (levels,) + tile, (levels,) + tile,
@@ -422,11 +492,17 @@
         (4, groups) + tile, (4, groups) + tile, (2, groups) + tile,
         (6,) + tile, (2, 6) + tile, (6, 8, 256), (6, 8 * tiles, 256),
         (2,) + tile, (2, 2) + tile, (2, 8, 256), (2, 8 * tiles, 256),
-        (levels,) + tile, (4, levels) + tile,
+        (levels,) + tile, (4, levels) + tile, tile, tile,
+    ]
+    staged = [
+        pltpu.VMEM(velocity.shape, F32), pltpu.VMEM(tracers.shape, F32), pltpu.VMEM(mixing.shape, F32),
+        pltpu.SMEM(thickness.shape, F32), pltpu.SMEM(coriolis.shape, F32),
+        pltpu.VMEM(land.shape, jnp.int32), pltpu.VMEM(bottom.shape, jnp.int32),
+        pltpu.VMEM(surface.shape, F32), pltpu.VMEM(barotropic.shape, F32),
     ]
     vmem = pl.BlockSpec(memory_space=pltpu.VMEM)
-    smem = pl.BlockSpec(memory_space=pltpu.SMEM)
-    return pl.pallas_call(
+    far = pl.BlockSpec(memory_space=pltpu.HBM)
+    results = pl.pallas_call(
         functools.partial(kernel, nx, ngy, nga, levels),
         out_shape=(
             jax.ShapeDtypeStruct(velocity.shape, F32),
@@ -434,14 +510,24 @@
             jax.ShapeDtypeStruct(surface.shape, F32),
             jax.ShapeDtypeStruct(barotropic.shape, F32),
         ),
-        in_specs=[vmem, vmem, vmem, smem, smem, vmem, vmem, vmem, vmem],
+        in_specs=[far] * 9,
         out_specs=(vmem, vmem, vmem, vmem),
         scratch_shapes=[pltpu.VMEM(s, F32) for s in scratch]
-        + [pltpu.SemaphoreType.DMA((copies,)), pltpu.SemaphoreType.DMA((copies,))],
+        + staged
+        + [pltpu.SemaphoreType.DMA((copies,)), pltpu.SemaphoreType.DMA((copies,)), pltpu.SemaphoreType.DMA((9,))],
         compiler_params=pltpu.CompilerParams(
-            collective_id=0, has_side_effects=True, vmem_limit_bytes=40 * 1024 * 1024
+            collective_id=0, has_side_effects=True, vmem_limit_bytes=64 * 1024 * 1024
         ),
     )(velocity, tracers, mixing, thickness, coriolis, land, bottom, surface, barotropic)
+    anywhere = pl.BlockSpec(memory_space=pltpu.HBM)
+    return pl.pallas_call(
+        settle,
+        out_shape=tuple(jax.ShapeDtypeStruct(r.shape, r.dtype) for r in results),
+        in_specs=[anywhere] * 4,
+        out_specs=(anywhere,) * 4,
+        scratch_shapes=[pltpu.SemaphoreType.DMA((4,))],
+        compiler_params=pltpu.CompilerParams(vmem_limit_bytes=64 * 1024 * 1024),
+    )(*results)
 
 
 def solution(mesh):

time: 67.6 us -> 87.9 us (1.30)
  Pallas kernels: 56.5 us -> 87.1 us
  local copies, waits for them, and re-layouts: 10.1 us -> 0 us
    pallas_call x0 -> x1, Pallas kernels: none -> 41.2 us  [shards(): pl.pallas_call(settle, out_shape=tuple((jax.ShapeDtypeStruct(r.shape, r.d...]
    pallas_call x1, Pallas kernels: 56.5 us -> 45.9 us  [shards(): pl.pallas_call(functools.partial(kernel, nx, ngy, nga, levels), out_shape...]
    unnamed x22 -> x0, local copies, waits for them, and re-layouts: 10.1 us -> none
where the time goes in v1:
time: 87.9 us; the launch traced here: 87.7 us
  Pallas kernels  87.1 us (99%)
    pallas_call x1, Pallas kernels, shards(): pl.pallas_call(functools.partial(kernel, nx, ngy, nga, levels), out_shape...  45.9 us
    pallas_call x1, Pallas kernels, shards(): pl.pallas_call(settle, out_shape=tuple((jax.ShapeDtypeStruct(r.shape, r.d...  41.2 us

profile of v1, /device:TPU:0, one launch (start us, length us, event | category | flops | bytes accessed | tf_op | source)
XLA Modules:
  0.0 87.7 jit_solution(12682052349716975874)
XLA Ops:
  0.6 45.9 %shard_map.120 = (f32[2,80,8,128]{3,2,1,0:T(8,128)}, f32[2,80,8,128]{3,2,1,0:T(8,128)}, f32[8,128]{1,0:T(8,128)}, f32[2,8,128]{2,1,0:T(8,128)}) custom-call(f32[2,80,8,128]{3,2,1,0:T(8,128)} %vel_in.1, f32[2,80,8,128]{3,2,1,0:T(8,128)} %trc_in.1, f32[80,8,128]{2,1,0:T(8,128)} %mix_in.1, f32[80]{0:T(128)} %dz_in.1, f32[8]{0:T(128)} %cor_in.1, ...), custom_call_target="tpu_custom_call" | custom-call | tf_op jit(solution)/shard_map/pallas_call | solution.py:505
  46.5 41.2 %shard_map.121 = (f32[2,80,8,128]{3,2,1,0:T(8,128)}, f32[2,80,8,128]{3,2,1,0:T(8,128)}, f32[8,128]{1,0:T(8,128)}, f32[2,8,128]{2,1,0:T(8,128)}) custom-call(f32[2,80,8,128]{3,2,1,0:T(8,128)} %get-tuple-element.8.refs_0_, f32[2,80,8,128]{3,2,1,0:T(8,128)} %get-tuple-element.9.refs_1_, f32[8,128]{1,0:T(8,128)} %get-tuple-element.10.refs_2_, ...), custom_call_target="tpu_custom_call" | custom-call | tf_op jit(solution)/shard_map/pallas_call | solution.py:523

commit v2 on v1

--- a/solution.py
+++ b/solution.py
@@ -19,7 +19,7 @@
     ynorth, ysouth, hnorth, hsouth,
     xpack, xrecv, crn, crs, bq, bl, bcorn,
     tile2, t2recv, wide1, all1, push1, p2recv, wide2, all2,
-    ratio_buf, val_buf, be_above, be_below,
+    ratio_buf, val_buf, be_above, be_below, state, fixed, high, flow,
     vel, trc, mix, dz, cor, land, bot, surf, baro,
     send_sem, recv_sem, load_sem,
 ):
@@ -101,9 +101,8 @@
     tile2[0] = surf[...]
     tile2[1] = baro[0]
     tile2[2] = baro[1]
-    tile2[3] = be
-    tile2[4] = depth_sum / jnp.broadcast_to(dz_total, (8, 128))
-    tile2[5] = rot
+    tile2[3] = depth_sum / jnp.broadcast_to(dz_total, (8, 128))
+    tile2[4] = be
 
     pl.semaphore_wait(
         barrier, 2 + tiles - 1 + jnp.where(has_n, 2, 0) + jnp.where(has_s, 2, 0)
@@ -136,15 +135,15 @@
             i = nxt()
             to = lax.rem(t + p, tiles)
             origin = lax.rem(t + tiles - p, tiles)
-            starts.append(rc(src, dst.at[:, rows_of(t), :], i, dev(gx, to)))
-            waits.append(rc(src, dst.at[:, rows_of(origin), :], i, dev(gx, to)))
+            starts.append(rc(src, dst.at[t], i, dev(gx, to)))
+            waits.append(rc(src, dst.at[origin], i, dev(gx, to)))
         return starts, waits
 
     two_d = pair(tile2, t2recv)
     for c in two_d:
         c.start()
-    be_up = rc(tile2.at[3], be_below, nxt(), dev(gx, up))
-    be_down = rc(tile2.at[3], be_above, nxt(), dev(gx, down))
+    be_up = rc(tile2.at[4], be_below, nxt(), dev(gx, up))
+    be_down = rc(tile2.at[4], be_above, nxt(), dev(gx, down))
     pl.when(has_n)(be_up.start)
     pl.when(has_s)(be_down.start)
     for c in loads[6:8]:
@@ -167,32 +166,45 @@
     def field(c, k):
         return vel[c, k] if c < 2 else trc[c - 2, k]
 
-    def pack_body(n, carry):
-        acc = [jnp.zeros((8, 128), F32)] * 6
-        for i in range(BLOCK):
-            k = n * BLOCK + i
-            wet = k.astype(F32) < be
-            q = [jnp.where(wet, field(c, k), 0.0) for c in range(4)]
-            yn = jnp.concatenate([a[6:8] for a in q], axis=0)
-            ys = jnp.concatenate([a[0:2] for a in q], axis=0)
-            ynorth[k] = yn
-            ysouth[k] = ys
-            here = slot == i
-            for c, a in enumerate(q + [yn, ys]):
-                acc[c] = jnp.where(here, pltpu.roll(a, 2 + 4 * i, 1), acc[c])
+    def masked(k):
+        wet = k.astype(F32) < be
+        return [jnp.where(wet, field(c, k), 0.0) for c in range(4)]
+
+    def place(n, first, acc):
         g = n // per_group
         part = n - per_group * g
         here = slot // BLOCK == part
-        for c in range(6):
-            xpack[c, g] = jnp.where(
-                here, pltpu.roll(acc[c], 4 * BLOCK * part, 1), xpack[c, g]
+        for j, a in enumerate(acc):
+            xpack[first + j, g] = jnp.where(
+                here, pltpu.roll(a, 4 * BLOCK * part, 1), xpack[first + j, g]
             )
+
+    def pack_rows(n, carry):
+        acc = [jnp.zeros((8, 128), F32)] * 2
+        for i in range(BLOCK):
+            k = n * BLOCK + i
+            q = masked(k)
+            ends = [
+                jnp.concatenate([a[6:8] for a in q], axis=0),
+                jnp.concatenate([a[0:2] for a in q], axis=0),
+            ]
+            ynorth[k] = ends[0]
+            ysouth[k] = ends[1]
+            for c in range(2):
+                acc[c] = jnp.where(slot == i, pltpu.roll(ends[c], 2 + 4 * i, 1), acc[c])
+        place(n, 4, acc)
         return carry
 
-    lax.fori_loop(0, blocks, pack_body, 0)
-    x_copies = pair(xpack.at[pl.ds(0, 4)], xrecv)
-    for c in x_copies:
-        c.start()
+    def pack_columns(n, carry):
+        acc = [jnp.zeros((8, 128), F32)] * 4
+        for i in range(BLOCK):
+            q = masked(n * BLOCK + i)
+            for c in range(4):
+                acc[c] = jnp.where(slot == i, pltpu.roll(q[c], 2 + 4 * i, 1), acc[c])
+        place(n, 0, acc)
+        return carry
+
+    lax.fori_loop(0, blocks, pack_rows, 0)
     diag_n = [
         rc(xpack.at[4], crs.at[1], nxt(), dev(left, up)),
         rc(xpack.at[4], crs.at[0], nxt(), dev(right, up)),
@@ -221,20 +233,40 @@
         pl.when(has_n)(to_north(n).start)
         pl.when(has_s)(to_south(n).start)
 
+    lax.fori_loop(0, blocks, pack_columns, 0)
+    x_copies = pair(xpack.at[pl.ds(0, 4)], xrecv)
+    for c in x_copies:
+        c.start()
+
     for c in two_d:
         c.wait_recv()
-    for f in range(6):
-        wide1[f, :, 0:128] = tile2[f]
-        wide1[f, :, 128:256] = jnp.where(lane < 64, t2recv[1, f], t2recv[0, f])
-    starts1, waits1 = peers(wide1, all1)
+    for f in range(4):
+        wide1[2 * f] = tile2[f]
+        wide1[2 * f + 1] = jnp.where(lane < 64, t2recv[1, f], t2recv[0, f])
+    wide1[8] = rot
+    all1[t] = wide1[...]
+    core = lax.rem(t // nga, 2)
+    stride = 2 * nga
+    chips = tiles // 2
+    my_chip = (t // stride) * nga + lax.rem(t, nga)
+
+    def tile_of(chip, on):
+        return (chip // nga) * stride + on * nga + lax.rem(chip, nga)
+
+    starts1, waits1 = [], []
+    for p in range(1, chips):
+        i = nxt()
+        to = dev(gx, tile_of(lax.rem(my_chip + p, chips), core))
+        origin = tile_of(lax.rem(my_chip + chips - p, chips), core)
+        starts1.append(rc(wide1, all1.at[t], i, to))
+        waits1.append(rc(wide1, all1.at[origin], i, to))
     for c in starts1:
         c.start()
-    all1[:, rows_of(t), :] = wide1[...]
 
     be_side = jnp.where(
         l4 == 1,
-        jnp.broadcast_to(t2recv[0, 3][:, 127:128], (8, 128)),
-        jnp.broadcast_to(t2recv[1, 3][:, 0:1], (8, 128)),
+        jnp.broadcast_to(t2recv[0, 4][:, 127:128], (8, 128)),
+        jnp.broadcast_to(t2recv[1, 4][:, 0:1], (8, 128)),
     )
     for c in x_copies:
         c.wait_recv()
@@ -370,11 +402,22 @@
 
     carry = lax.fori_loop(0, blocks, block_body, carry)
 
+    for c in waits1:
+        c.wait_recv()
+    hand, handed = [], []
+    for chip in range(chips):
+        i = nxt()
+        mate = dev(gx, tile_of(my_chip, 1 - core))
+        have, want = tile_of(chip, core), tile_of(chip, 1 - core)
+        hand.append(rc(all1.at[have], all1.at[have], i, mate))
+        handed.append(rc(all1.at[want], all1.at[want], i, mate))
     scale = land_f / safe
     push1[0] = carry[2] * scale
     push1[1] = carry[3] * scale
     push_copies = pair(push1, p2recv)
     for c in push_copies:
+        c.start()
+    for c in hand:
         c.start()
 
     def back_body(n, state):
@@ -394,59 +437,80 @@
         return after, mean_u, mean_v
 
     half = blocks // 3
-    state = lax.fori_loop(0, half, back_body, ((zero,) * 4, zero, zero))
+    solved = lax.fori_loop(0, half, back_body, ((zero,) * 4, zero, zero))
     for c in push_copies:
         c.wait_recv()
     for f in range(2):
-        wide2[f, :, 0:128] = push1[f]
-        wide2[f, :, 128:256] = jnp.where(lane < 64, p2recv[1, f], p2recv[0, f])
+        wide2[2 * f] = push1[f]
+        wide2[2 * f + 1] = jnp.where(lane < 64, p2recv[1, f], p2recv[0, f])
     starts2, waits2 = peers(wide2, all2)
     for c in starts2:
         c.start()
-    all2[:, rows_of(t), :] = wide2[...]
-    state = lax.fori_loop(half, blocks, back_body, state)
-    unused, mean_u, mean_v = state
-
-    shape = (8 * tiles, 256)
-    rows = lax.broadcasted_iota(jnp.int32, shape, 0)
-    top, base = rows == shape[0] - 1, rows == 0
-    for c in waits1:
+    all2[t] = wide2[...]
+    unused, mean_u, mean_v = lax.fori_loop(half, blocks, back_body, solved)
+
+    count = 8 * tiles
+    shape = (count, 128)
+    lanes = lax.broadcasted_iota(jnp.int32, shape, 1)
+    at_first, at_last = lanes == 0, lanes == 127
+    for c in handed:
         c.wait_recv()
-    sea = jnp.where(all1[3] >= 0.0, 1.0, 0.0)
-    ratio_x = 0.05 * all1[4]
+    body = pl.ds(8, count)
+    above, below = pl.ds(9, count), pl.ds(7, count)
+    for ref in (high, flow):
+        for h in range(2):
+            ref[h, 0:8, :] = jnp.zeros((8, 128), F32)
+            ref[h, count + 8:count + 16, :] = jnp.zeros((8, 128), F32)
     for c in waits2:
         c.wait_recv()
-    all1[3] = sea
-    all1[4] = ratio_x
-    all1[5] = 0.1 * all1[5] * sea
-    all2[0] = 0.1 * all2[0] * sea
-    all2[1] = 0.1 * all2[1] * sea
+    for tile in range(tiles):
+        at = slice(8 * tile, 8 * tile + 8)
+        f = all1[tile, 8]
+        for h in range(2):
+            depth = all1[tile, 6 + h]
+            sea = jnp.where(depth > 0.0, 1.0, 0.0)
+            state[0, h, at] = all1[tile, h]
+            state[1, h, at] = all1[tile, 2 + h]
+            state[2, h, at] = all1[tile, 4 + h]
+            fixed[0, h, at] = sea
+            fixed[1, h, at] = 0.05 * depth
+            fixed[2, h, at] = 0.1 * f * sea
+            fixed[3, h, at] = 0.1 * all2[tile, h] * sea
+            fixed[4, h, at] = 0.1 * all2[tile, 2 + h] * sea
     mine = rows_of(t)
 
     def diff_x(a):
-        return pltpu.roll(a, 255, 1) - pltpu.roll(a, 1, 1)
-
-    def diff_y(a):
-        return jnp.where(top, 0.0, pltpu.roll(a, shape[0] - 1, 0)) - jnp.where(
-            base, 0.0, pltpu.roll(a, 1, 0)
-        )
+        e = [pltpu.roll(x, 127, 1) for x in a]
+        w = [pltpu.roll(x, 1, 1) for x in a]
+        return [
+            jnp.where(at_last, e[1 - h], e[h]) - jnp.where(at_first, w[1 - h], w[h])
+            for h in range(2)
+        ]
 
     def sub_body(i, sums):
-        height, u, v = all1[0], all1[1], all1[2]
-        sea, dr, f = all1[3], all1[4], all1[5]
-        height = (height - (diff_x(dr * u) + diff_y(dr * v))) * sea
-        g = 1.25 * sea
-        new_u = u * sea + all2[0] + f * v - g * diff_x(height)
-        new_v = v * sea + all2[1] - f * u - g * diff_y(height)
-        all1[0] = height
-        all1[1] = new_u
-        all1[2] = new_v
-        return sums[0] + all1[1, mine, 0:128], sums[1] + all1[2, mine, 0:128]
+        u = [state[1, h] for h in range(2)]
+        v = [state[2, h] for h in range(2)]
+        for h in range(2):
+            flow[h, body] = fixed[1, h] * v[h]
+        dx = diff_x([fixed[1, h] * u[h] for h in range(2)])
+        tall = []
+        for h in range(2):
+            dy = flow[h, above] - flow[h, below]
+            tall.append((state[0, h] - (dx[h] + dy)) * fixed[0, h])
+            high[h, body] = tall[h]
+            state[0, h] = tall[h]
+        dx = diff_x(tall)
+        for h in range(2):
+            sea, f = fixed[0, h], fixed[2, h]
+            g = 1.25 * sea
+            state[1, h] = u[h] * sea + fixed[3, h] + f * v[h] - g * dx[h]
+            state[2, h] = v[h] * sea + fixed[4, h] - f * u[h] - g * (high[h, above] - high[h, below])
+        return sums[0] + state[1, 0, mine], sums[1] + state[2, 0, mine]
 
     sum_u, sum_v = lax.fori_loop(0, NSUB, sub_body, (zero, zero))
-    surf_out[...] = all1[0, mine, 0:128]
-    baro_out[0] = all1[1, mine, 0:128]
-    baro_out[1] = all1[2, mine, 0:128]
+    surf_out[...] = state[0, 0, mine]
+    baro_out[0] = state[1, 0, mine]
+    baro_out[1] = state[2, 0, mine]
     shift_u = sum_u * (1.0 / NSUB) - mean_u / safe
     shift_v = sum_v * (1.0 / NSUB) - mean_v / safe
 
@@ -460,7 +524,7 @@
 
     lax.fori_loop(0, blocks, out_body, 0)
 
-    for c in two_d + x_copies + starts1 + push_copies + starts2:
+    for c in two_d + x_copies + starts1 + hand + push_copies + starts2:
         c.wait_send()
     norths = diag_n + [be_up] + [to_north(n) for n in range(blocks)]
     souths = diag_s + [be_down] + [to_south(n) for n in range(blocks)]
@@ -470,14 +534,26 @@
         pl.when(has_s)(c.wait_send)
 
 
-def settle(*refs):
-    count = len(refs) // 2
-    sem = refs[-1]
-    copies = [pltpu.make_async_copy(refs[i], refs[count + i], sem.at[i]) for i in range(count)]
-    for c in copies:
-        c.start()
-    for c in copies:
+def settle(vel_in, trc_in, surf_in, baro_in, vel_out, trc_out, surf_out, baro_out,
+           vel, trc, surf, baro, in_sem, out_sem):
+    levels = vel_in.shape[1]
+    half = levels // 2
+    trips = []
+    for src, mid, dst in ((vel_in, vel, vel_out), (trc_in, trc, trc_out)):
+        for c in range(2):
+            for at in (pl.ds(0, half), pl.ds(half, levels - half)):
+                trips.append((src.at[c, at], mid.at[c, at], dst.at[c, at]))
+    trips.append((surf_in, surf, surf_out))
+    trips.append((baro_in, baro, baro_out))
+    ins = [pltpu.make_async_copy(s, m, in_sem.at[i]) for i, (s, m, d) in enumerate(trips)]
+    outs = [pltpu.make_async_copy(m, d, out_sem.at[i]) for i, (s, m, d) in enumerate(trips)]
+    for c in ins:
+        c.start()
+    for c, o in zip(ins, outs):
         c.wait()
+        o.start()
+    for o in outs:
+        o.wait()
 
 
 def shards(nx, ngy, nga, velocity, tracers, mixing, thickness, coriolis, land, bottom, surface, barotropic):
@@ -490,9 +566,10 @@
         (levels,) + tile, (levels,) + tile, (levels,) + tile, (levels,) + tile,
         (6, groups) + tile, (2, 4, groups) + tile, (2, groups) + tile, (2, groups) + tile,
         (4, groups) + tile, (4, groups) + tile, (2, groups) + tile,
-        (6,) + tile, (2, 6) + tile, (6, 8, 256), (6, 8 * tiles, 256),
-        (2,) + tile, (2, 2) + tile, (2, 8, 256), (2, 8 * tiles, 256),
+        (5,) + tile, (2, 5) + tile, (9,) + tile, (tiles, 9) + tile,
+        (2,) + tile, (2, 2) + tile, (4,) + tile, (tiles, 4) + tile,
         (levels,) + tile, (4, levels) + tile, tile, tile,
+        (3, 2, 8 * tiles, 128), (5, 2, 8 * tiles, 128), (2, 8 * tiles + 16, 128), (2, 8 * tiles + 16, 128),
     ]
     staged = [
         pltpu.VMEM(velocity.shape, F32), pltpu.VMEM(tracers.shape, F32), pltpu.VMEM(mixing.shape, F32),
@@ -525,7 +602,8 @@
         out_shape=tuple(jax.ShapeDtypeStruct(r.shape, r.dtype) for r in results),
         in_specs=[anywhere] * 4,
         out_specs=(anywhere,) * 4,
-        scratch_shapes=[pltpu.SemaphoreType.DMA((4,))],
+        scratch_shapes=[pltpu.VMEM(r.shape, F32) for r in results]
+        + [pltpu.SemaphoreType.DMA((10,)), pltpu.SemaphoreType.DMA((10,))],
         compiler_params=pltpu.CompilerParams(vmem_limit_bytes=64 * 1024 * 1024),
     )(*results)
 

time: 87.9 us -> 47.5 us (0.54)
  Pallas kernels: 87.1 us -> 46.7 us
    pallas_call x1, Pallas kernels: 41.2 us -> 2.24 us  [shards(): pl.pallas_call(settle, out_shape=tuple((jax.ShapeDtypeStruct(r.shape, r.d...]
    pallas_call x1, Pallas kernels: 45.9 us -> 44.5 us  [shards(): pl.pallas_call(functools.partial(kernel, nx, ngy, nga, levels), out_shape...]
where the time goes in v2:
time: 47.5 us; the launch traced here: 47.4 us
  Pallas kernels  46.7 us (98%)
  between operations  0.64 us (1%)
    pallas_call x1, Pallas kernels, shards(): pl.pallas_call(functools.partial(kernel, nx, ngy, nga, levels), out_shape...  44.5 us
    pallas_call x1, Pallas kernels, shards(): pl.pallas_call(settle, out_shape=tuple((jax.ShapeDtypeStruct(r.shape, r.d...  2.24 us

profile of v2, /device:TPU:0, one launch (start us, length us, event | category | flops | bytes accessed | tf_op | source)
XLA Modules:
  0.0 47.4 jit_solution(6745111268041334083)
XLA Ops:
  0.6 44.5 %shard_map.120 = (f32[2,80,8,128]{3,2,1,0:T(8,128)}, f32[2,80,8,128]{3,2,1,0:T(8,128)}, f32[8,128]{1,0:T(8,128)}, f32[2,8,128]{2,1,0:T(8,128)}) custom-call(f32[2,80,8,128]{3,2,1,0:T(8,128)} %vel_in.1, f32[2,80,8,128]{3,2,1,0:T(8,128)} %trc_in.1, f32[80,8,128]{2,1,0:T(8,128)} %mix_in.1, f32[80]{0:T(128)} %dz_in.1, f32[8]{0:T(128)} %cor_in.1, ...), custom_call_target="tpu_custom_call" | custom-call | tf_op jit(solution)/shard_map/pallas_call | solution.py:582
  45.1 2.2 %shard_map.121 = (f32[2,80,8,128]{3,2,1,0:T(8,128)}, f32[2,80,8,128]{3,2,1,0:T(8,128)}, f32[8,128]{1,0:T(8,128)}, f32[2,8,128]{2,1,0:T(8,128)}) custom-call(f32[2,80,8,128]{3,2,1,0:T(8,128)} %get-tuple-element.8.vel_in, f32[2,80,8,128]{3,2,1,0:T(8,128)} %get-tuple-element.9.trc_in, f32[8,128]{1,0:T(8,128)} %get-tuple-element.10.surf_in, ...), custom_call_target="tpu_custom_call" | custom-call | tf_op jit(solution)/shard_map/pallas_call | solution.py:600

commit v3 on v2

--- a/solution.py
+++ b/solution.py
@@ -15,7 +15,7 @@
 def kernel(
     nx, ngy, nga, levels,
     vel_in, trc_in, mix_in, dz_in, cor_in, land_in, bot_in, surf_in, baro_in,
-    vel_out, trc_out, surf_out, baro_out,
+    solved_out, small_out,
     ynorth, ysouth, hnorth, hsouth,
     xpack, xrecv, crn, crs, bq, bl, bcorn,
     tile2, t2recv, wide1, all1, push1, p2recv, wide2, all2,
@@ -31,9 +31,15 @@
         pltpu.make_async_copy(src, dst, load_sem.at[i])
         for i, (src, dst) in enumerate([
             (dz_in, dz), (cor_in, cor), (land_in, land), (bot_in, bot), (surf_in, surf),
-            (baro_in, baro), (vel_in, vel), (trc_in, trc), (mix_in, mix),
-        ])
+            (baro_in, baro),
+        ] + [
+            (src.at[c, pl.ds(at, levels // 2)], dst.at[c, pl.ds(at, levels // 2)])
+            for at in (0, levels // 2)
+            for src, dst in ((vel_in, vel), (trc_in, trc))
+            for c in range(2)
+        ] + [(mix_in, mix)])
     ]
+    count_loads = len(loads)
     for c in loads:
         c.start()
     gx = lax.axis_index("gx")
@@ -146,8 +152,6 @@
     be_down = rc(tile2.at[4], be_above, nxt(), dev(gx, down))
     pl.when(has_n)(be_up.start)
     pl.when(has_s)(be_down.start)
-    for c in loads[6:8]:
-        c.wait()
 
     @pl.when(jnp.logical_not(has_n))
     def _():
@@ -193,6 +197,8 @@
             for c in range(2):
                 acc[c] = jnp.where(slot == i, pltpu.roll(ends[c], 2 + 4 * i, 1), acc[c])
         place(n, 4, acc)
+        pl.when(has_n)(lambda: to_north(n).start())
+        pl.when(has_s)(lambda: to_south(n).start())
         return carry
 
     def pack_columns(n, carry):
@@ -204,7 +210,23 @@
         place(n, 0, acc)
         return carry
 
-    lax.fori_loop(0, blocks, pack_rows, 0)
+    first_north, first_south = index[0], index[0] + blocks
+    index[0] += 2 * blocks
+
+    def to_north(n):
+        span = pl.ds(n * BLOCK, BLOCK)
+        return rc(ynorth.at[span], hsouth.at[span], first_north + n, dev(gx, up))
+
+    def to_south(n):
+        span = pl.ds(n * BLOCK, BLOCK)
+        return rc(ysouth.at[span], hnorth.at[span], first_south + n, dev(gx, down))
+
+    for c in loads[6:10]:
+        c.wait()
+    lax.fori_loop(0, blocks // 2, pack_rows, 0)
+    for c in loads[10:14]:
+        c.wait()
+    lax.fori_loop(blocks // 2, blocks, pack_rows, 0)
     diag_n = [
         rc(xpack.at[4], crs.at[1], nxt(), dev(left, up)),
         rc(xpack.at[4], crs.at[0], nxt(), dev(right, up)),
@@ -217,21 +239,6 @@
         pl.when(has_n)(c.start)
     for c in diag_s:
         pl.when(has_s)(c.start)
-
-    first_north, first_south = index[0], index[0] + blocks
-    index[0] += 2 * blocks
-
-    def to_north(n):
-        span = pl.ds(n * BLOCK, BLOCK)
-        return rc(ynorth.at[span], hsouth.at[span], first_north + n, dev(gx, up))
-
-    def to_south(n):
-        span = pl.ds(n * BLOCK, BLOCK)
-        return rc(ysouth.at[span], hnorth.at[span], first_south + n, dev(gx, down))
-
-    for n in range(blocks):
-        pl.when(has_n)(to_north(n).start)
-        pl.when(has_s)(to_south(n).start)
 
     lax.fori_loop(0, blocks, pack_columns, 0)
     x_copies = pair(xpack.at[pl.ds(0, 4)], xrecv)
@@ -305,7 +312,7 @@
 
     pl.when(has_s)(be_up.wait_recv)
     pl.when(has_n)(be_down.wait_recv)
-    loads[8].wait()
+    loads[14].wait()
     be_n = jnp.broadcast_to(be_above[0:1, :], (8, 128))
     be_s = jnp.broadcast_to(be_below[7:8, :], (8, 128))
 
@@ -428,8 +435,8 @@
             now = [val_buf[c, k] + ratio * after[c] for c in range(4)]
             val_buf[0, k] = now[0]
             val_buf[1, k] = now[1]
-            trc_out[0, k] = now[2]
-            trc_out[1, k] = now[3]
+            val_buf[2, k] = now[2]
+            val_buf[3, k] = now[3]
             part = jnp.where(k.astype(F32) < be, dz[k], 0.0)
             mean_u = mean_u + part * now[0]
             mean_v = mean_v + part * now[1]
@@ -448,6 +455,12 @@
         c.start()
     all2[t] = wide2[...]
     unused, mean_u, mean_v = lax.fori_loop(half, blocks, back_body, solved)
+    leaving = [
+        pltpu.make_async_copy(val_buf.at[c], solved_out.at[c], load_sem.at[count_loads + c])
+        for c in range(4)
+    ]
+    for c in leaving:
+        c.start()
 
     count = 8 * tiles
     shape = (count, 128)
@@ -508,22 +521,15 @@
         return sums[0] + state[1, 0, mine], sums[1] + state[2, 0, mine]
 
     sum_u, sum_v = lax.fori_loop(0, NSUB, sub_body, (zero, zero))
-    surf_out[...] = state[0, 0, mine]
-    baro_out[0] = state[1, 0, mine]
-    baro_out[1] = state[2, 0, mine]
-    shift_u = sum_u * (1.0 / NSUB) - mean_u / safe
-    shift_v = sum_v * (1.0 / NSUB) - mean_v / safe
-
-    def out_body(n, carry):
-        for i in range(BLOCK):
-            k = n * BLOCK + i
-            wet = k.astype(F32) < be
-            vel_out[0, k] = jnp.where(wet, val_buf[0, k] + shift_u, 0.0)
-            vel_out[1, k] = jnp.where(wet, val_buf[1, k] + shift_v, 0.0)
-        return carry
-
-    lax.fori_loop(0, blocks, out_body, 0)
-
+    small_out[0] = state[0, 0, mine]
+    small_out[1] = state[1, 0, mine]
+    small_out[2] = state[2, 0, mine]
+    small_out[3] = sum_u * (1.0 / NSUB) - mean_u / safe
+    small_out[4] = sum_v * (1.0 / NSUB) - mean_v / safe
+    small_out[5] = be
+
+    for c in leaving:
+        c.wait()
     for c in two_d + x_copies + starts1 + hand + push_copies + starts2:
         c.wait_send()
     norths = diag_n + [be_up] + [to_north(n) for n in range(blocks)]
@@ -534,26 +540,46 @@
         pl.when(has_s)(c.wait_send)
 
 
-def settle(vel_in, trc_in, surf_in, baro_in, vel_out, trc_out, surf_out, baro_out,
-           vel, trc, surf, baro, in_sem, out_sem):
-    levels = vel_in.shape[1]
+def settle(solved_in, small_in, vel_out, trc_out, surf_out, baro_out,
+           solved, small, in_sem, out_sem):
+    levels = solved_in.shape[1]
     half = levels // 2
+    first = pltpu.make_async_copy(small_in, small, in_sem.at[0])
+    first.start()
     trips = []
-    for src, mid, dst in ((vel_in, vel, vel_out), (trc_in, trc, trc_out)):
-        for c in range(2):
-            for at in (pl.ds(0, half), pl.ds(half, levels - half)):
-                trips.append((src.at[c, at], mid.at[c, at], dst.at[c, at]))
-    trips.append((surf_in, surf, surf_out))
-    trips.append((baro_in, baro, baro_out))
-    ins = [pltpu.make_async_copy(s, m, in_sem.at[i]) for i, (s, m, d) in enumerate(trips)]
-    outs = [pltpu.make_async_copy(m, d, out_sem.at[i]) for i, (s, m, d) in enumerate(trips)]
+    for c in range(4):
+        dst = vel_out if c < 2 else trc_out
+        for at in (0, half):
+            span = pl.ds(at, half)
+            trips.append((c, at, solved_in.at[c, span], solved.at[c, span], dst.at[c % 2, span]))
+    ins = [pltpu.make_async_copy(x[2], x[3], in_sem.at[1 + i]) for i, x in enumerate(trips)]
+    outs = [pltpu.make_async_copy(x[3], x[4], out_sem.at[2 + i]) for i, x in enumerate(trips)]
+    ends = [
+        pltpu.make_async_copy(small.at[0], surf_out, out_sem.at[0]),
+        pltpu.make_async_copy(small.at[pl.ds(1, 2)], baro_out, out_sem.at[1]),
+    ]
     for c in ins:
         c.start()
-    for c, o in zip(ins, outs):
+    first.wait()
+    for c in ends:
+        c.start()
+    be = small[5]
+    for i, (c, at, *unused) in enumerate(trips):
+        ins[i].wait()
+        if c < 2:
+            shift = small[3 + c]
+
+            def body(n, carry):
+                for j in range(BLOCK):
+                    k = at + n * BLOCK + j
+                    wet = k.astype(F32) < be
+                    solved[c, k] = jnp.where(wet, solved[c, k] + shift, 0.0)
+                return carry
+
+            lax.fori_loop(0, half // BLOCK, body, 0)
+        outs[i].start()
+    for c in ends + outs:
         c.wait()
-        o.start()
-    for o in outs:
-        o.wait()
 
 
 def shards(nx, ngy, nga, velocity, tracers, mixing, thickness, coriolis, land, bottom, surface, barotropic):
@@ -582,16 +608,14 @@
     results = pl.pallas_call(
         functools.partial(kernel, nx, ngy, nga, levels),
         out_shape=(
-            jax.ShapeDtypeStruct(velocity.shape, F32),
-            jax.ShapeDtypeStruct(tracers.shape, F32),
-            jax.ShapeDtypeStruct(surface.shape, F32),
-            jax.ShapeDtypeStruct(barotropic.shape, F32),
+            jax.ShapeDtypeStruct((4, levels) + tile, F32),
+            jax.ShapeDtypeStruct((6,) + tile, F32),
         ),
         in_specs=[far] * 9,
-        out_specs=(vmem, vmem, vmem, vmem),
+        out_specs=(far, vmem),
         scratch_shapes=[pltpu.VMEM(s, F32) for s in scratch]
         + staged
-        + [pltpu.SemaphoreType.DMA((copies,)), pltpu.SemaphoreType.DMA((copies,)), pltpu.SemaphoreType.DMA((9,))],
+        + [pltpu.SemaphoreType.DMA((copies,)), pltpu.SemaphoreType.DMA((copies,)), pltpu.SemaphoreType.DMA((19,))],
         compiler_params=pltpu.CompilerParams(
             collective_id=0, has_side_effects=True, vmem_limit_bytes=64 * 1024 * 1024
         ),
@@ -599,8 +623,10 @@
     anywhere = pl.BlockSpec(memory_space=pltpu.HBM)
     return pl.pallas_call(
         settle,
-        out_shape=tuple(jax.ShapeDtypeStruct(r.shape, r.dtype) for r in results),
-        in_specs=[anywhere] * 4,
+        out_shape=tuple(
+            jax.ShapeDtypeStruct(r.shape, F32) for r in (velocity, tracers, surface, barotropic)
+        ),
+        in_specs=[anywhere] * 2,
         out_specs=(anywhere,) * 4,
         scratch_shapes=[pltpu.VMEM(r.shape, F32) for r in results]
         + [pltpu.SemaphoreType.DMA((10,)), pltpu.SemaphoreType.DMA((10,))],

time: 47.5 us -> 45.8 us (0.964)
  Pallas kernels: 46.7 us -> 45 us
    pallas_call x1, Pallas kernels: 44.5 us -> 42.7 us  [shards(): pl.pallas_call(functools.partial(kernel, nx, ngy, nga, levels), out_shape...]
where the time goes in v3:
time: 45.8 us; the launch traced here: 45.6 us
  Pallas kernels  45 us (98%)
  between operations  0.64 us (1%)
    pallas_call x1, Pallas kernels, shards(): pl.pallas_call(functools.partial(kernel, nx, ngy, nga, levels), out_shape...  42.7 us
    pallas_call x1, Pallas kernels, shards(): pl.pallas_call(settle, out_shape=tuple((jax.ShapeDtypeStruct(r.shape, F32...  2.27 us

profile of v3, /device:TPU:0, one launch (start us, length us, event | category | flops | bytes accessed | tf_op | source)
XLA Modules:
  0.0 45.6 jit_solution(5241355847118503306)
XLA Ops:
  0.6 42.7 %shard_map.120 = (f32[4,80,8,128]{3,2,1,0:T(8,128)}, f32[6,8,128]{2,1,0:T(8,128)}) custom-call(f32[2,80,8,128]{3,2,1,0:T(8,128)} %vel_in.1, f32[2,80,8,128]{3,2,1,0:T(8,128)} %trc_in.1, f32[80,8,128]{2,1,0:T(8,128)} %mix_in.1, f32[80]{0:T(128)} %dz_in.1, f32[8]{0:T(128)} %cor_in.1, s32[8,128]{1,0:T(8,128)} %land_in.1, s32[8,128]{1,0:T(8,128)} %bot_in.1, ...), custom_call_target="tpu_custom_call" | custom-call | tf_op jit(solution)/shard_map/pallas_call | solution.py:608
  43.3 2.3 %shard_map.121 = (f32[2,80,8,128]{3,2,1,0:T(8,128)}, f32[2,80,8,128]{3,2,1,0:T(8,128)}, f32[8,128]{1,0:T(8,128)}, f32[2,8,128]{2,1,0:T(8,128)}) custom-call(f32[4,80,8,128]{3,2,1,0:T(8,128)} %get-tuple-element.6.solved_in, f32[6,8,128]{2,1,0:T(8,128)} %get-tuple-element.7.small_in), custom_call_target="tpu_custom_call" | custom-call | tf_op jit(solution)/shard_map/pallas_call | solution.py:624

commit v4 on v3

--- a/solution.py
+++ b/solution.py
@@ -199,6 +199,10 @@
         place(n, 4, acc)
         pl.when(has_n)(lambda: to_north(n).start())
         pl.when(has_s)(lambda: to_south(n).start())
+        g = n // per_group
+        full = jnp.logical_or(n - per_group * g == per_group - 1, n == blocks - 1)
+        pl.when(jnp.logical_and(full, has_n))(lambda: start_all(diag_n(g)))
+        pl.when(jnp.logical_and(full, has_s))(lambda: start_all(diag_s(g)))
         return carry
 
     def pack_columns(n, carry):
@@ -211,7 +215,30 @@
         return carry
 
     first_north, first_south = index[0], index[0] + blocks
-    index[0] += 2 * blocks
+    first_diag = index[0] + 2 * blocks
+    index[0] += 2 * blocks + 4 * groups
+
+    def diag_n(g):
+        i = first_diag + g
+        return [
+            rc(xpack.at[4, g], crs.at[1, g], i, dev(left, up)),
+            rc(xpack.at[4, g], crs.at[0, g], i + groups, dev(right, up)),
+        ]
+
+    def diag_s(g):
+        i = first_diag + 2 * groups + g
+        return [
+            rc(xpack.at[5, g], crn.at[1, g], i, dev(left, down)),
+            rc(xpack.at[5, g], crn.at[0, g], i + groups, dev(right, down)),
+        ]
+
+    def start_all(copies):
+        for c in copies:
+            c.start()
+
+    def recv_all(copies):
+        for c in copies:
+            c.wait_recv()
 
     def to_north(n):
         span = pl.ds(n * BLOCK, BLOCK)
@@ -227,19 +254,6 @@
     for c in loads[10:14]:
         c.wait()
     lax.fori_loop(blocks // 2, blocks, pack_rows, 0)
-    diag_n = [
-        rc(xpack.at[4], crs.at[1], nxt(), dev(left, up)),
-        rc(xpack.at[4], crs.at[0], nxt(), dev(right, up)),
-    ]
-    diag_s = [
-        rc(xpack.at[5], crn.at[1], nxt(), dev(left, down)),
-        rc(xpack.at[5], crn.at[0], nxt(), dev(right, down)),
-    ]
-    for c in diag_n:
-        pl.when(has_n)(c.start)
-    for c in diag_s:
-        pl.when(has_s)(c.start)
-
     lax.fori_loop(0, blocks, pack_columns, 0)
     x_copies = pair(xpack.at[pl.ds(0, 4)], xrecv)
     for c in x_copies:
@@ -277,16 +291,15 @@
     )
     for c in x_copies:
         c.wait_recv()
-    for c in diag_n:
-        pl.when(has_s)(c.wait_recv)
-    for c in diag_s:
-        pl.when(has_n)(c.wait_recv)
 
     def close(a):
         return jnp.where(l4 == 1, a, pltpu.roll(a, 126, 1))
 
     low = l4 < 2
-    for g in range(groups):
+
+    def open_group(g):
+        pl.when(has_s)(lambda: recv_all(diag_n(g)))
+        pl.when(has_n)(lambda: recv_all(diag_s(g)))
         corner_n = jnp.where(low, crn[0, g], crn[1, g])
         corner_s = jnp.where(low, crs[0, g], crs[1, g])
         bcorn[0, g] = close(corner_n)
@@ -395,6 +408,7 @@
 
     def block_body(n, carry):
         g = n // per_group
+        pl.when(n == per_group * g)(lambda: open_group(g))
         back = lax.rem(128 - 4 * BLOCK * (n - per_group * g), 128)
         rims = (
             [pltpu.roll(bq[c, g], back, 1) for c in range(4)],
@@ -483,9 +497,10 @@
             depth = all1[tile, 6 + h]
             sea = jnp.where(depth > 0.0, 1.0, 0.0)
             state[0, h, at] = all1[tile, h]
-            state[1, h, at] = all1[tile, 2 + h]
-            state[2, h, at] = all1[tile, 4 + h]
+            state[1, h, at] = all1[tile, 2 + h] * sea
+            state[2, h, at] = all1[tile, 4 + h] * sea
             fixed[0, h, at] = sea
+            fixed[5, h, at] = 1.25 * sea
             fixed[1, h, at] = 0.05 * depth
             fixed[2, h, at] = 0.1 * f * sea
             fixed[3, h, at] = 0.1 * all2[tile, h] * sea
@@ -514,10 +529,9 @@
             state[0, h] = tall[h]
         dx = diff_x(tall)
         for h in range(2):
-            sea, f = fixed[0, h], fixed[2, h]
-            g = 1.25 * sea
-            state[1, h] = u[h] * sea + fixed[3, h] + f * v[h] - g * dx[h]
-            state[2, h] = v[h] * sea + fixed[4, h] - f * u[h] - g * (high[h, above] - high[h, below])
+            f, g = fixed[2, h], fixed[5, h]
+            state[1, h] = u[h] + fixed[3, h] + f * v[h] - g * dx[h]
+            state[2, h] = v[h] + fixed[4, h] - f * u[h] - g * (high[h, above] - high[h, below])
         return sums[0] + state[1, 0, mine], sums[1] + state[2, 0, mine]
 
     sum_u, sum_v = lax.fori_loop(0, NSUB, sub_body, (zero, zero))
@@ -532,8 +546,8 @@
         c.wait()
     for c in two_d + x_copies + starts1 + hand + push_copies + starts2:
         c.wait_send()
-    norths = diag_n + [be_up] + [to_north(n) for n in range(blocks)]
-    souths = diag_s + [be_down] + [to_south(n) for n in range(blocks)]
+    norths = sum([diag_n(g) for g in range(groups)], []) + [be_up] + [to_north(n) for n in range(blocks)]
+    souths = sum([diag_s(g) for g in range(groups)], []) + [be_down] + [to_south(n) for n in range(blocks)]
     for c in norths:
         pl.when(has_n)(c.wait_send)
     for c in souths:
@@ -586,7 +600,7 @@
     levels = thickness.shape[0]
     tiles = ngy * nga
     groups = (levels + 31) // 32
-    copies = 4 + 2 * (levels // BLOCK) + 2 + 4 + (tiles - 1) + 2 + (tiles - 1)
+    copies = 4 + 2 * (levels // BLOCK) + 2 + 4 * groups + (tiles - 1) + 2 + (tiles - 1)
     tile = (8, 128)
     scratch = [
         (levels,) + tile, (levels,) + tile, (levels,) + tile, (levels,) + tile,
@@ -595,7 +609,7 @@
         (5,) + tile, (2, 5) + tile, (9,) + tile, (tiles, 9) + tile,
         (2,) + tile, (2, 2) + tile, (4,) + tile, (tiles, 4) + tile,
         (levels,) + tile, (4, levels) + tile, tile, tile,
-        (3, 2, 8 * tiles, 128), (5, 2, 8 * tiles, 128), (2, 8 * tiles + 16, 128), (2, 8 * tiles + 16, 128),
+        (3, 2, 8 * tiles, 128), (6, 2, 8 * tiles, 128), (2, 8 * tiles + 16, 128), (2, 8 * tiles + 16, 128),
     ]
     staged = [
         pltpu.VMEM(velocity.shape, F32), pltpu.VMEM(tracers.shape, F32), pltpu.VMEM(mixing.shape, F32),

time: 45.8 us -> 46.1 us (level)
  no operation moved by 1% of the time
where the time goes in v4:
time: 46.1 us; the launch traced here: 46 us
  Pallas kernels  45.3 us (98%)
  between operations  0.64 us (1%)
    pallas_call x1, Pallas kernels, shards(): pl.pallas_call(functools.partial(kernel, nx, ngy, nga, levels), out_shape...  43.1 us
    pallas_call x1, Pallas kernels, shards(): pl.pallas_call(settle, out_shape=tuple((jax.ShapeDtypeStruct(r.shape, F32...  2.27 us

profile of v4, /device:TPU:0, one launch (start us, length us, event | category | flops | bytes accessed | tf_op | source)
XLA Modules:
  0.0 46.0 jit_solution(10353411603903695427)
XLA Ops:
  0.6 43.1 %shard_map.120 = (f32[4,80,8,128]{3,2,1,0:T(8,128)}, f32[6,8,128]{2,1,0:T(8,128)}) custom-call(f32[2,80,8,128]{3,2,1,0:T(8,128)} %vel_in.1, f32[2,80,8,128]{3,2,1,0:T(8,128)} %trc_in.1, f32[80,8,128]{2,1,0:T(8,128)} %mix_in.1, f32[80]{0:T(128)} %dz_in.1, f32[8]{0:T(128)} %cor_in.1, s32[8,128]{1,0:T(8,128)} %land_in.1, s32[8,128]{1,0:T(8,128)} %bot_in.1, ...), custom_call_target="tpu_custom_call" | custom-call | tf_op jit(solution)/shard_map/pallas_call | solution.py:622
  43.7 2.3 %shard_map.121 = (f32[2,80,8,128]{3,2,1,0:T(8,128)}, f32[2,80,8,128]{3,2,1,0:T(8,128)}, f32[8,128]{1,0:T(8,128)}, f32[2,8,128]{2,1,0:T(8,128)}) custom-call(f32[4,80,8,128]{3,2,1,0:T(8,128)} %get-tuple-element.6.solved_in, f32[6,8,128]{2,1,0:T(8,128)} %get-tuple-element.7.small_in), custom_call_target="tpu_custom_call" | custom-call | tf_op jit(solution)/shard_map/pallas_call | solution.py:638
